TPU v7x, 32 devices: a whole 2x2x4 slice. The times are simulated.
32 devices in a mesh: dp: 16 (over z, y, x), stream: 2 (over core).
Axes of the slice: x: 2, y: 2, z: 4, core: 2. Of those that a mesh axis runs over, the one named last changes fastest.
Arguments:
- tokens: bfloat16 [16384, 512], P(('dp', 'stream')), may hold values from -6 to 6
- memory: bfloat16 [16384, 512], P(('dp', 'stream')), may hold values from -6 to 6
- cotangent: bfloat16 [16384, 512], P(('dp', 'stream')), may hold values from -6 to 6
- segments: int32 [16384], P(('dp', 'stream')), may hold values from 0 to 1039, as said below
- padding: int32 [16384], P(('dp', 'stream')), may hold values from 0 to 1, as said below
- priority: int32 [16384], P(('dp', 'stream')), may hold values from 0 to 4095
- threshold: int32 [16384], P(('dp', 'stream')), may hold values from 0 to 4096
- master: float32 [8192, 512], P(('dp', 'stream'))
- momentum: float32 [8192, 512], P(('dp', 'stream')), may hold values from -80 to 80
- vectors: float32 [8704], replicated
- vec_first: float32 [8704], replicated, may hold values from -224 to 224
- vec_second: float32 [8704], replicated, may hold values from 1.47456 to 5.89824
- step_count: int32 [1], replicated, may hold values from 2 to 20
Outputs:
- layer_out: bfloat16 [16384, 512], P(('dp', 'stream'))
- input_grad: float32 [16384, 512], P(('dp', 'stream'))
- memory_grad: float32 [16384, 512], P(('dp', 'stream'))
- new_momentum: float32 [8192, 512], P(('dp', 'stream'))
- new_master: float32 [8192, 512], P(('dp', 'stream'))
- new_vectors: float32 [8704], replicated
- new_vec_first: float32 [8704], replicated
- new_vec_second: float32 [8704], replicated
Inputs may be any that keep to these rules, and one draw needn't show every extreme that they name: `segments`: ids never fall and never cross an aligned block of 1024 rows. A block holds one whole document of 1024 tokens (some blocks in every draw) or sentences of 16 to 44 tokens, whose last one may be cut off by the block's end. `padding`: 1 exactly on the rows of a sentence cut off by its block's end.
All inputs are finite; a program needn't handle non-finite values.
Results may differ from a plain program's by a relative error of at most 0.025.
The roundings to bfloat16 on the way count: a program that leaves them out, or rounds other values in their place, can miss the bound.
Values may be sent and summed in bfloat16 or wider, within the bound.
A program may use at most 256 MiB of HBM per device.

v0:
```python
import jax
import jax.numpy as jnp
from jax import lax
from jax.sharding import PartitionSpec as P

D = 512
HEADS = 8
HEAD = 64
FF = 2048


NS_A = 3.4445
NS_B = -4.775
NS_C = 2.0315
MUON_RATE = 0.8
ADAM_RATE = 0.2
ADAM_DECAY = 0.01
HIGH = lax.Precision.HIGHEST


def partner(block, axis, stride):
    count = lax.axis_size(axis)
    route = []
    for low in range(count):
        high = low | 1 << stride
        if high != low and high < count:
            route += [(low, high), (high, low)]
    return lax.ppermute(block, axis, route)


def plain_dot(left_mat, right_mat):
    return jnp.dot(left_mat, right_mat, preferred_element_type=jnp.float32)


def lead_dot(left_mat, right_mat):
    return lax.dot_general(
        left_mat, right_mat, (((0,), (0,)), ((), ())), preferred_element_type=jnp.float32
    )


def last_dot(left_mat, right_mat):
    return lax.dot_general(
        left_mat, right_mat, (((1,), (1,)), ((), ())), preferred_element_type=jnp.float32
    )


def exact_dot(left_mat, right_mat):
    return jnp.dot(left_mat, right_mat, precision=HIGH)


def exact_lead(left_mat, right_mat):
    return lax.dot_general(left_mat, right_mat, (((0,), (0,)), ((), ())), precision=HIGH)


def split_rows(all_rows):
    attn_w = all_rows[: 8 * D].reshape(8, D, D)
    return (attn_w, all_rows[8 * D : 8 * D + FF], all_rows[8 * D + FF :])


def norm_forward(values, gain_vec, shift_vec):
    center = values - jnp.mean(values, axis=-1, keepdims=True)
    spread = lax.rsqrt(jnp.mean(center * center, axis=-1, keepdims=True) + 1e-05)
    normed = center * spread
    return (normed * gain_vec + shift_vec, normed, spread)


def norm_backward(normed, spread, gain_vec, grad_out):
    grad_gain = jnp.sum(grad_out * normed, axis=0)
    grad_shift = jnp.sum(grad_out, axis=0)
    scaled = grad_out * gain_vec
    grad_in = spread * (
        scaled
        - jnp.mean(scaled, axis=-1, keepdims=True)
        - normed * jnp.mean(scaled * normed, axis=-1, keepdims=True)
    )
    return (grad_in, grad_gain, grad_shift)


def split_heads(matrix):
    return matrix.reshape(matrix.shape[0], HEADS, HEAD)


def block_scores(queries, keys_all, visible):
    scores = jnp.einsum(
        "qhe,khe->hqk",
        split_heads(queries),
        split_heads(keys_all),
        preferred_element_type=jnp.float32,
    )
    return jnp.where(visible[None], scores * HEAD ** (-0.5), -1e30)


def attend_forward(queries, keys_all, values_all, visible):
    scores = block_scores(queries, keys_all, visible)
    row_max = jnp.max(scores, axis=-1, keepdims=True)
    expo = jnp.exp(scores - row_max)
    row_total = jnp.sum(expo, axis=-1, keepdims=True)
    weights_low = (expo / row_total).astype(jnp.bfloat16)
    mixed = jnp.einsum(
        "hqk,khe->qhe", weights_low, split_heads(values_all), preferred_element_type=jnp.float32
    )
    return (mixed.reshape(queries.shape[0], HEADS * HEAD), row_max + jnp.log(row_total))


def attend_backward(queries, keys_all, values_all, visible, logsum, grad_out):
    probs = jnp.exp(block_scores(queries, keys_all, visible) - logsum)
    grad_heads = split_heads(grad_out)
    grad_probs = jnp.einsum(
        "qhe,khe->hqk", grad_heads, split_heads(values_all), preferred_element_type=jnp.float32
    )
    inner_sum = jnp.sum(grad_probs * probs, axis=-1, keepdims=True)
    grad_scores = (probs * (grad_probs - inner_sum) * HEAD ** (-0.5)).astype(jnp.bfloat16)
    grad_q = jnp.einsum(
        "hqk,khe->qhe", grad_scores, split_heads(keys_all), preferred_element_type=jnp.float32
    )
    grad_k = jnp.einsum(
        "hqk,qhe->khe", grad_scores, split_heads(queries), preferred_element_type=jnp.float32
    )
    grad_v = jnp.einsum(
        "hqk,qhe->khe", probs.astype(jnp.bfloat16), grad_heads, preferred_element_type=jnp.float32
    )
    key_count = keys_all.shape[0]
    return (
        grad_q.reshape(queries.shape[0], HEADS * HEAD),
        grad_k.reshape(key_count, HEADS * HEAD),
        grad_v.reshape(key_count, HEADS * HEAD),
    )


def attend_all(queries, keys_all, values_all, visible):
    mixed, logsum = attend_forward(queries, keys_all, values_all, visible)
    logsums = [logsum]
    return (mixed, logsums)


def attend_back_all(queries, keys_all, values_all, visible, logsums, grad_out):
    block_rows = min(512, queries.shape[0])
    grad_q_parts = []
    grad_keys = jnp.zeros(keys_all.shape, jnp.float32)
    grad_values = jnp.zeros(values_all.shape, jnp.float32)
    for block_index, begin_row in enumerate(range(0, queries.shape[0], block_rows)):
        grad_q, grad_k, grad_v = attend_backward(
            queries, keys_all, values_all, visible, logsums[block_index], grad_out
        )
        grad_q_parts.append(grad_q)
        grad_keys = grad_k
        grad_values = grad_v
    return (grad_q_parts[0], grad_keys, grad_values)


def per_device(
    tokens,
    memory,
    cotangent,
    segments,
    padding,
    priority,
    threshold,
    master,
    momentum,
    vectors,
    vec_first,
    vec_second,
    step_count,
):

    def vector_part(position):
        return vectors[position * D : (position + 1) * D]

    low_master = master.astype(jnp.bfloat16)
    attn_w, w_in, w_out = split_rows(
        lax.all_gather(low_master, ("dp", "stream"), axis=0, tiled=True)
    )
    tokens_f32 = tokens.astype(jnp.float32)
    ln_one, normed_one, spread_one = norm_forward(tokens_f32, vector_part(0), vector_part(1))
    h_one = ln_one.astype(jnp.bfloat16)
    queries = (plain_dot(h_one, attn_w[0]) + vector_part(6)).astype(jnp.bfloat16)
    keys_own = plain_dot(h_one, attn_w[1]).astype(jnp.bfloat16)
    values_own = (plain_dot(h_one, attn_w[2]) + vector_part(7)).astype(jnp.bfloat16)
    mem_keys = plain_dot(memory, attn_w[5]).astype(jnp.bfloat16)
    mem_values = (plain_dot(memory, attn_w[6]) + vector_part(10)).astype(jnp.bfloat16)
    keys_all, values_all, mem_keys_all, mem_values_all = (
        lax.all_gather(keys_own, "stream", axis=0, tiled=True),
        lax.all_gather(values_own, "stream", axis=0, tiled=True),
        lax.all_gather(mem_keys, "stream", axis=0, tiled=True),
        lax.all_gather(mem_values, "stream", axis=0, tiled=True),
    )
    seg_all, pad_all, prio_all = (
        lax.all_gather(segments, "stream", axis=0, tiled=True),
        lax.all_gather(padding, "stream", axis=0, tiled=True),
        lax.all_gather(priority, "stream", axis=0, tiled=True),
    )
    own_rows = queries.shape[0]
    place = jnp.arange(own_rows, dtype=jnp.int32) + lax.axis_index("stream") * own_rows
    key_place = jnp.arange(seg_all.shape[0], dtype=jnp.int32)
    diagonal = place[:, None] == key_place[None, :]
    same_seg = segments[:, None] == seg_all[None, :]
    open_key = (pad_all == 0)[None, :]
    vis_self = same_seg & ((prio_all[None, :] < threshold[:, None]) & open_key | diagonal)
    vis_cross = same_seg & (open_key | diagonal)
    attn_out, lse_one = attend_all(queries, keys_all, values_all, vis_self)
    attn_low = attn_out.astype(jnp.bfloat16)
    res_one = tokens_f32 + plain_dot(attn_low, attn_w[3]) + vector_part(8)
    ln_two, normed_two, spread_two = norm_forward(res_one, vector_part(2), vector_part(3))
    h_two = ln_two.astype(jnp.bfloat16)
    cross_q = (plain_dot(h_two, attn_w[4]) + vector_part(9)).astype(jnp.bfloat16)
    cross_out, lse_two = attend_all(cross_q, mem_keys_all, mem_values_all, vis_cross)
    cross_low = cross_out.astype(jnp.bfloat16)
    res_two = res_one + plain_dot(cross_low, attn_w[7]) + vector_part(11)
    ln_three, normed_three, spread_three = norm_forward(res_two, vector_part(4), vector_part(5))
    h_three = ln_three.astype(jnp.bfloat16)
    pre_act = last_dot(h_three, w_in) + vectors[13 * D :]
    hidden = jnp.maximum(pre_act, 0.0).astype(jnp.bfloat16)
    layer_out = (res_two + plain_dot(hidden, w_out) + vector_part(12)).astype(jnp.bfloat16)
    grad_out_w = lead_dot(hidden, cotangent)
    grad_bias_out = jnp.sum(cotangent.astype(jnp.float32), axis=0)
    grad_hidden = last_dot(cotangent, w_out)
    grad_pre = jnp.where(pre_act > 0, grad_hidden, 0.0).astype(jnp.bfloat16)
    grad_bias_hidden = jnp.sum(grad_pre.astype(jnp.float32), axis=0)
    grad_in_w = lead_dot(grad_pre, h_three)
    grad_ln_three, grad_gain_three, grad_shift_three = norm_backward(
        normed_three, spread_three, vector_part(4), plain_dot(grad_pre, w_in)
    )
    grad_res_two = cotangent.astype(jnp.float32) + grad_ln_three
    grad_res_two_low = grad_res_two.astype(jnp.bfloat16)
    grad_bias_cross_o = jnp.sum(grad_res_two, axis=0)
    grad_cross_o_w = lead_dot(cross_low, grad_res_two_low)
    grad_cross = last_dot(grad_res_two_low, attn_w[7]).astype(jnp.bfloat16)
    grad_cq, grad_mk_all, grad_mv_all = attend_back_all(
        cross_q, mem_keys_all, mem_values_all, vis_cross, lse_two, grad_cross
    )
    grad_cq_low = grad_cq.astype(jnp.bfloat16)
    grad_bias_cq = jnp.sum(grad_cq_low.astype(jnp.float32), axis=0)
    grad_cq_w = lead_dot(h_two, grad_cq_low)
    grad_ln_two, grad_gain_two, grad_shift_two = norm_backward(
        normed_two, spread_two, vector_part(2), last_dot(grad_cq_low, attn_w[4])
    )
    grad_res_one = grad_res_two + grad_ln_two
    grad_res_one_low = grad_res_one.astype(jnp.bfloat16)
    grad_bias_o = jnp.sum(grad_res_one, axis=0)
    grad_o_w = lead_dot(attn_low, grad_res_one_low)
    grad_attn = last_dot(grad_res_one_low, attn_w[3]).astype(jnp.bfloat16)
    grad_q, grad_k_all, grad_v_all = attend_back_all(
        queries, keys_all, values_all, vis_self, lse_one, grad_attn
    )
    grad_k, grad_v, grad_mk, grad_mv = (
        lax.psum_scatter(grad_k_all, "stream", scatter_dimension=0, tiled=True),
        lax.psum_scatter(grad_v_all, "stream", scatter_dimension=0, tiled=True),
        lax.psum_scatter(grad_mk_all, "stream", scatter_dimension=0, tiled=True),
        lax.psum_scatter(grad_mv_all, "stream", scatter_dimension=0, tiled=True),
    )
    grad_q_low = grad_q.astype(jnp.bfloat16)
    grad_k_low = grad_k.astype(jnp.bfloat16)
    grad_v_low = grad_v.astype(jnp.bfloat16)
    grad_mk_low = grad_mk.astype(jnp.bfloat16)
    grad_mv_low = grad_mv.astype(jnp.bfloat16)
    grad_h_one = (
        last_dot(grad_q_low, attn_w[0])
        + last_dot(grad_k_low, attn_w[1])
        + last_dot(grad_v_low, attn_w[2])
    )
    grad_ln_one, grad_gain_one, grad_shift_one = norm_backward(
        normed_one, spread_one, vector_part(0), grad_h_one
    )
    input_grad = grad_res_one + grad_ln_one
    memory_grad = last_dot(grad_mk_low, attn_w[5]) + last_dot(grad_mv_low, attn_w[6])
    stacked = jnp.concatenate(
        [
            lead_dot(h_one, grad_q_low),
            lead_dot(h_one, grad_k_low),
            lead_dot(h_one, grad_v_low),
            grad_o_w,
            grad_cq_w,
            lead_dot(memory, grad_mk_low),
            lead_dot(memory, grad_mv_low),
            grad_cross_o_w,
            grad_in_w,
            grad_out_w,
        ],
        axis=0,
    )
    vec_local = jnp.concatenate(
        [
            grad_gain_one,
            grad_shift_one,
            grad_gain_two,
            grad_shift_two,
            grad_gain_three,
            grad_shift_three,
            jnp.sum(grad_q_low.astype(jnp.float32), axis=0),
            jnp.sum(grad_v_low.astype(jnp.float32), axis=0),
            grad_bias_o,
            grad_bias_cq,
            jnp.sum(grad_mv_low.astype(jnp.float32), axis=0),
            grad_bias_cross_o,
            grad_bias_out,
            grad_bias_hidden,
        ],
        axis=0,
    )
    grad_rows = lax.psum_scatter(stacked, ("dp", "stream"), scatter_dimension=0, tiled=True)
    grad_vec = lax.psum(vec_local, ("dp", "stream"))
    opt_rows = master.shape[0]
    device_index = lax.axis_index(("dp", "stream"))
    start_row = device_index * opt_rows
    in_ffn = start_row >= 8 * D
    att_bits = (D // opt_rows).bit_length() - 1
    ffn_bits = (FF // opt_rows).bit_length() - 1
    own_bits = jnp.where(in_ffn, ffn_bits, att_bits)
    new_momentum = 0.5 * momentum + grad_rows

    def gram_total(partial_value):
        for bit_pos in range(ffn_bits):
            other = partner(partial_value, ("dp", "stream"), bit_pos)
            partial_value = partial_value + jnp.where(bit_pos < own_bits, other, 0.0)
        return partial_value

    gram_first = gram_total(exact_lead(new_momentum, new_momentum))
    divisor = jnp.sqrt(jnp.trace(gram_first)) + 1e-07
    current = new_momentum / divisor
    gram = gram_first / (divisor * divisor)
    for turn in range(5):
        if turn > 0:
            gram = gram_total(exact_lead(current, current))
        poly = NS_B * gram + NS_C * exact_dot(gram, gram)
        current = NS_A * current + exact_dot(current, poly)
    rate = MUON_RATE * jnp.where(in_ffn, (FF / D) ** 0.5, 1.0)
    new_master = master - rate * current
    count = step_count[0].astype(jnp.float32)
    new_first = 0.5 * vec_first + 0.5 * grad_vec
    new_second = 0.999 * vec_second + 0.001 * grad_vec * grad_vec
    first_fix = new_first / (1.0 - jnp.power(0.5, count))
    second_fix = new_second / (1.0 - jnp.power(0.999, count))
    new_vectors = vectors - ADAM_RATE * (
        first_fix / (jnp.sqrt(second_fix) + 1e-08) + ADAM_DECAY * vectors
    )
    return (
        layer_out,
        input_grad,
        memory_grad,
        new_momentum,
        new_master,
        new_vectors,
        new_first,
        new_second,
    )


def solution(mesh):
    return jax.shard_map(
        per_device,
        mesh=mesh,
        in_specs=(
            P(("dp", "stream"), None),
            P(("dp", "stream"), None),
            P(("dp", "stream"), None),
            P(("dp", "stream")),
            P(("dp", "stream")),
            P(("dp", "stream")),
            P(("dp", "stream")),
            P(("dp", "stream"), None),
            P(("dp", "stream"), None),
            P(),
            P(),
            P(),
            P(),
        ),
        out_specs=(
            P(("dp", "stream"), None),
            P(("dp", "stream"), None),
            P(("dp", "stream"), None),
            P(("dp", "stream"), None),
            P(("dp", "stream"), None),
            P(),
            P(),
            P(),
        ),
        check_vma=False,
    )
```

profile of v0, /device:TPU:0, one launch (start us, length us, event | category | flops | bytes accessed | tf_op | source)
XLA Modules:
  0.0 939.5 jit_solution(10107269463332756582)
XLA Ops:
  12.1 79.5 %all-gather.9.cloned.1.call-done = bf16[8192,512]{1,0:T(8,128)(2,1)} async-done(((bf16[256,512]{1,0:T(8,128)(2,1)}), bf16[8192,512]{1,0:T(8,128)(2,1)}) %all-gather.9.cloned.1.call-update) | async-done | bytes 8388624 | tf_op jit(solution)/shard_map/all_gather | solution.py:172
  119.5 6.1 copy-done.1
  130.9 8.2 fusion.77
  149.1 5.7 copy-done.2
  160.1 8.0 fusion.76
  192.7 9.3 fusion.186
  202.0 30.6 %convert_reduce_fusion.4 = (f32[8,64]{1,0:T(8,128)S(1)}, bf16[8,64,512]{2,1,0:T(8,128)(2,1)}) fusion(bf16[1024,8,64]{0,2,1:T(8,128)(2,1)} %bitcast.106, f32[8,512,1024]{2,1,0:T(8,128)} %fusion.186, f32[8,512,1024]{2,1,0:T(8,128)} %copy-done.2, f32[8,512]{1,0:T(8,128)S(1)} %log_add_fusion.1), kind=kOutput, calls=%fused_computation.122 | convolution fusion | flops 567022080 | bytes 35145728 | tf_op jit(solution)/shard_map/hqk,khe->qhe/dot_general | solution.py:113
  244.6 9.3 fusion.187
  253.9 30.9 %fusion.19 = f32[8,64,1024]{2,1,0:T(8,128)} fusion(bf16[512,8,64]{0,2,1:T(8,128)(2,1)} %bitcast.116, f32[8,512,1024]{2,1,0:T(8,128)} %fusion.187, f32[8,512,1024]{2,1,0:T(8,128)} %copy-done.1, f32[8,512]{1,0:T(8,128)S(1)} %log_add_fusion), kind=kOutput, calls=%fused_computation.22 | convolution fusion | flops 566236160 | bytes 36192256 | tf_op jit(solution)/shard_map/hqk,qhe->khe/dot_general | solution.py:116
  284.9 10.8 %fusion.24 = f32[8,64,1024]{2,1,0:T(8,128)} fusion(bf16[512,8,64]{0,2,1:T(8,128)(2,1)} %bitcast.102, f32[8,512,1024]{2,1,0:T(8,128)} %copy-done.1, f32[8,512]{1,0:T(8,128)S(1)} %log_add_fusion), kind=kOutput, calls=%fused_computation.24 | convolution fusion | flops 545259520 | bytes 19415040 | tf_op jit(solution)/shard_map/hqk,qhe->khe/dot_general | solution.py:119
  295.7 30.9 %fusion.13 = f32[8,64,1024]{2,1,0:T(8,128)} fusion(bf16[512,8,64]{0,2,1:T(8,128)(2,1)} %bitcast.118, f32[8,512,1024]{2,1,0:T(8,128)} %fusion.186, f32[8,512,1024]{2,1,0:T(8,128)} %copy-done.2, f32[8,512]{1,0:T(8,128)S(1)} %log_add_fusion.1), kind=kOutput, calls=%fused_computation.20 | convolution fusion | flops 566236160 | bytes 36192256 | tf_op jit(solution)/shard_map/hqk,qhe->khe/dot_general | solution.py:116
  326.7 10.7 %fusion.26 = f32[8,64,1024]{2,1,0:T(8,128)} fusion(bf16[512,8,64]{0,2,1:T(8,128)(2,1)} %bitcast.100, f32[8,512,1024]{2,1,0:T(8,128)} %copy-done.2, f32[8,512]{1,0:T(8,128)S(1)} %log_add_fusion.1), kind=kOutput, calls=%fused_computation.25 | convolution fusion | flops 545259520 | bytes 19415040 | tf_op jit(solution)/shard_map/hqk,qhe->khe/dot_general | solution.py:119
  337.5 30.9 %convert_reduce_fusion.6 = (f32[8,64]{1,0:T(8,128)S(1)}, bf16[8,64,512]{2,1,0:T(8,128)(2,1)}) fusion(bf16[1024,8,64]{0,2,1:T(8,128)(2,1)} %bitcast.104, f32[8,512,1024]{2,1,0:T(8,128)} %fusion.187, f32[8,512,1024]{2,1,0:T(8,128)} %copy-done.1, f32[8,512]{1,0:T(8,128)S(1)} %log_add_fusion), kind=kOutput, calls=%fused_computation.124 | convolution fusion | flops 567022080 | bytes 35145728 | tf_op jit(solution)/shard_map/hqk,khe->qhe/dot_general | solution.py:113
  400.6 181.4 %reduce-scatter.14.cloned.1.call-done = f32[256,512]{1,0:T(8,128)} async-done(((f32[8192,512]{1,0:T(8,128)}), f32[256,512]{1,0:T(8,128)}) %reduce-scatter.14.cloned.1.call-update) | async-done | bytes 524304 | tf_op jit(solution)/shard_map/reduce_scatter | solution.py:301
  591.6 24.8 %collective-permute-done.1 = f32[512,512]{1,0:T(8,128)} collective-permute-done((f32[512,512]{1,0:T(8,128)}, f32[512,512]{1,0:T(8,128)}, u32[]{:S(2)}, u32[]{:S(2)}) %collective-permute-start.1) | collective-permute-done | bytes 1048608 | tf_op jit(solution)/shard_map/ppermute | solution.py:28
  620.6 23.2 %collective-permute-done.2 = f32[512,512]{1,0:T(8,128)} collective-permute-done((f32[512,512]{1,0:T(8,128)}, f32[512,512]{1,0:T(8,128)}, u32[]{:S(2)}, u32[]{:S(2)}) %collective-permute-start.2) | collective-permute-done | bytes 1048608 | tf_op jit(solution)/shard_map/ppermute | solution.py:28
  658.0 24.8 %collective-permute-done.4 = f32[512,512]{1,0:T(8,128)S(1)} collective-permute-done((f32[512,512]{1,0:T(8,128)S(1)}, f32[512,512]{1,0:T(8,128)S(1)}, u32[]{:S(2)}, u32[]{:S(2)}) %collective-permute-start.4) | collective-permute-done | bytes 1048608 | tf_op jit(solution)/shard_map/ppermute | solution.py:28
  684.9 22.6 %collective-permute-done.5 = f32[512,512]{1,0:T(8,128)S(1)} collective-permute-done((f32[512,512]{1,0:T(8,128)S(1)}, f32[512,512]{1,0:T(8,128)S(1)}, u32[]{:S(2)}, u32[]{:S(2)}) %collective-permute-start.5) | collective-permute-done | bytes 1048608 | tf_op jit(solution)/shard_map/ppermute | solution.py:28
  715.2 24.8 %collective-permute-done.7 = f32[512,512]{1,0:T(8,128)S(1)} collective-permute-done((f32[512,512]{1,0:T(8,128)S(1)}, f32[512,512]{1,0:T(8,128)S(1)}, u32[]{:S(2)}, u32[]{:S(2)}) %collective-permute-start.7) | collective-permute-done | bytes 1048608 | tf_op jit(solution)/shard_map/ppermute | solution.py:28
  742.0 22.6 %collective-permute-done.8 = f32[512,512]{1,0:T(8,128)S(1)} collective-permute-done((f32[512,512]{1,0:T(8,128)S(1)}, f32[512,512]{1,0:T(8,128)S(1)}, u32[]{:S(2)}, u32[]{:S(2)}) %collective-permute-start.8) | collective-permute-done | bytes 1048608 | tf_op jit(solution)/shard_map/ppermute | solution.py:28
  783.7 15.4 %collective-permute-done.10 = f32[512,512]{1,0:T(8,128)} collective-permute-done((f32[512,512]{1,0:T(8,128)}, f32[512,512]{1,0:T(8,128)}, u32[]{:S(2)}, u32[]{:S(2)}) %collective-permute-start.10) | collective-permute-done | bytes 1048608 | tf_op jit(solution)/shard_map/ppermute | solution.py:28
  806.6 18.3 %collective-permute-done.11 = f32[512,512]{1,0:T(8,128)S(1)} collective-permute-done((f32[512,512]{1,0:T(8,128)S(1)}, f32[512,512]{1,0:T(8,128)S(1)}, u32[]{:S(2)}, u32[]{:S(2)}) %collective-permute-start.11) | collective-permute-done | bytes 1048608 | tf_op jit(solution)/shard_map/ppermute | solution.py:28
  840.9 60.9 %psum.7 = f32[8704]{0:T(1024)S(1)} all-reduce(f32[8704]{0:T(1024)S(1)} %constant_dynamic-update-slice_fusion.10), channel_id=1, replica_groups=mesh['dp'=16,'stream'=2] {'dp','stream'}, use_global_device_ids=true, to_apply=%region_38.39 | all-reduce | flops 8704 | bytes 69632 | tf_op jit(solution)/shard_map/psum | solution.py:302
  910.6 16.8 %collective-permute-done.14 = f32[512,512]{1,0:T(8,128)S(1)} collective-permute-done((f32[512,512]{1,0:T(8,128)S(1)}, f32[512,512]{1,0:T(8,128)S(1)}, u32[]{:S(2)}, u32[]{:S(2)}) %collective-permute-start.14) | collective-permute-done | bytes 1048608 | tf_op jit(solution)/shard_map/ppermute | solution.py:28
  (230 shorter events, 216.4 us)
Async XLA Ops:
  7.2 84.5 %all-gather.9.cloned.1.call-start = ((), (), s32[]{:S(2)}) async-start(), calls=%async_computation.5 | async-start | bytes 8650752 | tf_op jit(solution)/shard_map/all_gather | solution.py:172
  9.1 105.5 %all-gather.13.cloned.1.call-start = ((), (), s32[]{:S(2)}) async-start(), calls=%async_computation.7 | async-start | bytes 1572864 | tf_op jit(solution)/shard_map/all_gather | solution.py:183
  94.2 35.2 %all-gather.11.cloned.1.call-start = ((), (), s32[]{:S(2)}) async-start(), calls=%async_computation.6 | async-start | bytes 1572864 | tf_op jit(solution)/shard_map/all_gather | solution.py:184
  96.7 44.3 %all-gather.17.cloned.1.call-start = ((), (), s32[]{:S(2)}) async-start(), calls=%async_computation.9 | async-start | bytes 1572864 | tf_op jit(solution)/shard_map/all_gather | solution.py:185
  99.1 59.5 %all-gather.15.cloned.1.call-start = ((), (), s32[]{:S(2)}) async-start(), calls=%async_computation.8 | async-start | bytes 1572864 | tf_op jit(solution)/shard_map/all_gather | solution.py:186
  112.9 258.0 %reduce-scatter.6.cloned.1.call-start = ((), (), s32[]{:S(2)}) async-start(), calls=%async_computation.10 | async-start | bytes 3145728 | tf_op jit(solution)/shard_map/reduce_scatter | solution.py:247
  284.8 88.8 %reduce-scatter.8.cloned.1.call-start = ((), (), s32[]{:S(2)}) async-start(), calls=%async_computation.11 | async-start | bytes 3145728 | tf_op jit(solution)/shard_map/reduce_scatter | solution.py:248
  295.7 86.0 %reduce-scatter.10.cloned.1.call-start = ((), (), s32[]{:S(2)}) async-start(), calls=%async_computation.12 | async-start | bytes 3145728 | tf_op jit(solution)/shard_map/reduce_scatter | solution.py:249
  326.6 57.9 %reduce-scatter.12.cloned.1.call-start = ((), (), s32[]{:S(2)}) async-start(), calls=%async_computation.13 | async-start | bytes 3145728 | tf_op jit(solution)/shard_map/reduce_scatter | solution.py:250
  337.4 244.6 %reduce-scatter.14.cloned.1.call-start = ((), (), s32[]{:S(2)}) async-start(), calls=%async_computation.14 | async-start | bytes 17301504 | tf_op jit(solution)/shard_map/reduce_scatter | solution.py:301
  585.1 3.0 collective-permute-start
  590.9 25.5 %collective-permute-start.1 = (f32[512,512]{1,0:T(8,128)}, f32[512,512]{1,0:T(8,128)}, u32[]{:S(2)}, u32[]{:S(2)}) collective-permute-start(f32[512,512]{1,0:T(8,128)} %select_add_fusion.14), channel_id=1, source_target_pairs={{0,2},{2,0},{1,3},{3,1},{4,6},{6,4},{5,7},{7,5},{8,10},{10,8},{9,1... | collective-permute-start | bytes 3145736 | tf_op jit(solution)/shard_map/ppermute | solution.py:28
  618.8 25.0 %collective-permute-start.2 = (f32[512,512]{1,0:T(8,128)}, f32[512,512]{1,0:T(8,128)}, u32[]{:S(2)}, u32[]{:S(2)}) collective-permute-start(f32[512,512]{1,0:T(8,128)} %select_add_fusion.13), channel_id=1, source_target_pairs={{0,4},{4,0},{1,5},{5,1},{2,6},{6,2},{3,7},{7,3},{8,12},{12,8},{9,1... | collective-permute-start | bytes 3145736 | tf_op jit(solution)/shard_map/ppermute | solution.py:28
  654.4 2.9 collective-permute-start.3
  657.5 25.3 %collective-permute-start.4 = (f32[512,512]{1,0:T(8,128)S(1)}, f32[512,512]{1,0:T(8,128)S(1)}, u32[]{:S(2)}, u32[]{:S(2)}) collective-permute-start(f32[512,512]{1,0:T(8,128)S(1)} %select_add_fusion.11), channel_id=1, source_target_pairs={{0,2},{2,0},{1,3},{3,1},{4,6},{6,4},{5,7},{7,5},{8,10},{10,8},{9,1... | collective-permute-start | bytes 3145736 | tf_op jit(solution)/shard_map/ppermute | solution.py:28
  683.0 24.4 %collective-permute-start.5 = (f32[512,512]{1,0:T(8,128)S(1)}, f32[512,512]{1,0:T(8,128)S(1)}, u32[]{:S(2)}, u32[]{:S(2)}) collective-permute-start(f32[512,512]{1,0:T(8,128)S(1)} %select_add_fusion.10), channel_id=1, source_target_pairs={{0,4},{4,0},{1,5},{5,1},{2,6},{6,2},{3,7},{7,3},{8,12},{12,8},{9,1... | collective-permute-start | bytes 3145736 | tf_op jit(solution)/shard_map/ppermute | solution.py:28
  711.7 2.7 collective-permute-start.6
  714.7 25.3 %collective-permute-start.7 = (f32[512,512]{1,0:T(8,128)S(1)}, f32[512,512]{1,0:T(8,128)S(1)}, u32[]{:S(2)}, u32[]{:S(2)}) collective-permute-start(f32[512,512]{1,0:T(8,128)S(1)} %select_add_fusion.8), channel_id=1, source_target_pairs={{0,2},{2,0},{1,3},{3,1},{4,6},{6,4},{5,7},{7,5},{8,10},{10,8},{9,1... | collective-permute-start | bytes 3145736 | tf_op jit(solution)/shard_map/ppermute | solution.py:28
  740.2 24.4 %collective-permute-start.8 = (f32[512,512]{1,0:T(8,128)S(1)}, f32[512,512]{1,0:T(8,128)S(1)}, u32[]{:S(2)}, u32[]{:S(2)}) collective-permute-start(f32[512,512]{1,0:T(8,128)S(1)} %select_add_fusion.7), channel_id=1, source_target_pairs={{0,4},{4,0},{1,5},{5,1},{2,6},{6,2},{3,7},{7,3},{8,12},{12,8},{9,1... | collective-permute-start | bytes 3145736 | tf_op jit(solution)/shard_map/ppermute | solution.py:28
  773.5 25.5 %collective-permute-start.10 = (f32[512,512]{1,0:T(8,128)}, f32[512,512]{1,0:T(8,128)}, u32[]{:S(2)}, u32[]{:S(2)}) collective-permute-start(f32[512,512]{1,0:T(8,128)} %select_add_fusion.5), channel_id=1, source_target_pairs={{0,2},{2,0},{1,3},{3,1},{4,6},{6,4},{5,7},{7,5},{8,10},{10,8},{9,1... | collective-permute-start | bytes 3145736 | tf_op jit(solution)/shard_map/ppermute | solution.py:28
  800.5 24.4 %collective-permute-start.11 = (f32[512,512]{1,0:T(8,128)S(1)}, f32[512,512]{1,0:T(8,128)S(1)}, u32[]{:S(2)}, u32[]{:S(2)}) collective-permute-start(f32[512,512]{1,0:T(8,128)S(1)} %select_add_fusion.4), channel_id=1, source_target_pairs={{0,4},{4,0},{1,5},{5,1},{2,6},{6,2},{3,7},{7,3},{8,12},{12,8},{9,1... | collective-permute-start | bytes 3145736 | tf_op jit(solution)/shard_map/ppermute | solution.py:28
  832.1 5.4 collective-permute-start.12
  840.2 61.6 %collective-permute-start.13 = (f32[512,512]{1,0:T(8,128)}, f32[512,512]{1,0:T(8,128)}, u32[]{:S(2)}, u32[]{:S(2)}) collective-permute-start(f32[512,512]{1,0:T(8,128)} %select_add_fusion.2), channel_id=1, source_target_pairs={{0,2},{2,0},{1,3},{3,1},{4,6},{6,4},{5,7},{7,5},{8,10},{10,8},{9,1... | collective-permute-start | bytes 3145736 | tf_op jit(solution)/shard_map/ppermute | solution.py:28
  903.2 24.2 %collective-permute-start.14 = (f32[512,512]{1,0:T(8,128)S(1)}, f32[512,512]{1,0:T(8,128)S(1)}, u32[]{:S(2)}, u32[]{:S(2)}) collective-permute-start(f32[512,512]{1,0:T(8,128)S(1)} %select_add_fusion.1), channel_id=1, source_target_pairs={{0,4},{4,0},{1,5},{5,1},{2,6},{6,2},{3,7},{7,3},{8,12},{12,8},{9,1... | collective-permute-start | bytes 3145736 | tf_op jit(solution)/shard_map/ppermute | solution.py:28
  (31 other events, 1197.2 us)
Sparse Core Ops, SparseCore 0:
  11.4 80.1 all-gather.8
  94.3 7.6 all-gather.12
  104.1 10.1 all-gather.10
  116.3 10.1 all-gather.16
  128.5 10.1 all-gather.14
  285.0 7.8 reduce-scatter.5
  295.8 10.2 reduce-scatter.7
  326.7 7.8 reduce-scatter.9
  337.5 10.2 reduce-scatter.11
  400.7 181.2 reduce-scatter.13
where the time goes:
time: 945 us; the launch traced here: 939 us
  waiting for transfers between devices  465 us (49%)
  matrix products  295 us (31%)
  blocking collectives  66.6 us (7%)
  other arithmetic  42 us (4%)
  local copies, waits for them, and re-layouts  40.5 us (4%)
  between operations  16.7 us (2%)
  starting transfers between devices  12.9 us (1%)
    ppermute x15, waiting for transfers between devices, partner(): return lax.ppermute(block, axis, route)  204 us
    reduce_scatter x1, waiting for transfers between devices, per_device(): lax.psum_scatter(stacked, ('dp', 'stream'), scatter_dimension=0, tiled=True)  181 us
    all_gather x1, waiting for transfers between devices, per_device(): lax.all_gather(low_master, ('dp', 'stream'), axis=0, tiled=True)  79.5 us
    dot_general x2, matrix products, attend_backward(): jnp.einsum('hqk,qhe->khe', grad_scores, split_heads(queries), preferred_e...  61.8 us
    dot_general x2, matrix products, attend_backward(): jnp.einsum('hqk,khe->qhe', grad_scores, split_heads(keys_all), preferred_...  61.5 us
    psum x1, blocking collectives, per_device(): grad_vec = lax.psum(vec_local, ('dp', 'stream'))  60.9 us
    dot_general x10, matrix products, lead_dot(): lax.dot_general(left_mat, right_mat, (((0,), (0,)), ((), ())), preferred_...  32.2 us
    unnamed x77, local copies, waits for them, and re-layouts  28.4 us
  transfers between devices with their start and end apart: 25, of which 15 were waited for; matrix products, arithmetic and copies ran while one was open for 18% of the time, Pallas kernels for 0%

commit v1 on v0

--- a/solution.py
+++ b/solution.py
@@ -44,8 +44,8 @@
     )
 
 
-def exact_dot(left_mat, right_mat):
-    return jnp.dot(left_mat, right_mat, precision=HIGH)
+def high_dot(left_mat, right_mat):
+    return jnp.dot(left_mat, right_mat, precision=lax.Precision.HIGH)
 
 
 def exact_lead(left_mat, right_mat):
@@ -317,13 +317,15 @@
 
     gram_first = gram_total(exact_lead(new_momentum, new_momentum))
     divisor = jnp.sqrt(jnp.trace(gram_first)) + 1e-07
-    current = new_momentum / divisor
     gram = gram_first / (divisor * divisor)
+    unit = jnp.eye(D, dtype=jnp.float32)
+    chain = None
     for turn in range(5):
-        if turn > 0:
-            gram = gram_total(exact_lead(current, current))
-        poly = NS_B * gram + NS_C * exact_dot(gram, gram)
-        current = NS_A * current + exact_dot(current, poly)
+        poly = NS_A * unit + NS_B * gram + NS_C * high_dot(gram, gram)
+        chain = poly if chain is None else high_dot(chain, poly)
+        if turn < 4:
+            gram = high_dot(high_dot(gram, poly), poly)
+    current = high_dot(new_momentum / divisor, chain)
     rate = MUON_RATE * jnp.where(in_ffn, (FF / D) ** 0.5, 1.0)
     new_master = master - rate * current
     count = step_count[0].astype(jnp.float32)

time: 945 us -> 713 us (0.75)
  waiting for transfers between devices: 465 us -> 263 us
  other arithmetic: 42 us -> 30.2 us
    ppermute x15 -> x3, waiting for transfers between devices: 204 us -> 16.8 us  [partner(): return lax.ppermute(block, axis, route)]
    reduce_scatter x1, waiting for transfers between devices: 181 us -> 166 us  [per_device(): lax.psum_scatter(stacked, ('dp', 'stream'), scatter_dimension=0, tiled=True)]
    add x10 -> x2, other arithmetic: 12.9 us -> 2 us  [gram_total(): partial_value = partial_value + jnp.where(bit_pos < own_bits, other, 0.0)]
    dot_general x10 -> x18, matrix products: 21.4 us -> 19.1 us  [high_dot(): return jnp.dot(left_mat, right_mat, precision=lax.Precision.HIGH)]
    unnamed x77 -> x73, local copies, waits for them, and re-layouts: 28.4 us -> 27.6 us
  transfers between devices with their start and end apart: 25 -> 13, of which waited for: 15 -> 3; matrix products, arithmetic and copies ran while one was open for 18% -> 25% of each run, Pallas kernels for 0% -> 0%
where the time goes in v1:
time: 713 us; the launch traced here: 707 us
  matrix products  288 us (40%)
  waiting for transfers between devices  263 us (37%)
  blocking collectives  65.1 us (9%)
  local copies, waits for them, and re-layouts  39.6 us (6%)
  other arithmetic  30.2 us (4%)
  between operations  16.7 us (2%)
    reduce_scatter x1, waiting for transfers between devices, per_device(): lax.psum_scatter(stacked, ('dp', 'stream'), scatter_dimension=0, tiled=True)  166 us
    all_gather x1, waiting for transfers between devices, per_device(): lax.all_gather(low_master, ('dp', 'stream'), axis=0, tiled=True)  79.5 us
    dot_general x2, matrix products, attend_backward(): jnp.einsum('hqk,qhe->khe', grad_scores, split_heads(queries), preferred_e...  61.7 us
    dot_general x2, matrix products, attend_backward(): jnp.einsum('hqk,khe->qhe', grad_scores, split_heads(keys_all), preferred_...  61.4 us
    psum x1, blocking collectives, per_device(): grad_vec = lax.psum(vec_local, ('dp', 'stream'))  59.4 us
    dot_general x10, matrix products, lead_dot(): lax.dot_general(left_mat, right_mat, (((0,), (0,)), ((), ())), preferred_...  32.2 us
    unnamed x73, local copies, waits for them, and re-layouts  27.6 us
    dot_general x10, matrix products, plain_dot(): return jnp.dot(left_mat, right_mat, preferred_element_type=jnp.float32)  25.5 us
  transfers between devices with their start and end apart: 13, of which 3 were waited for; matrix products, arithmetic and copies ran while one was open for 25% of the time, Pallas kernels for 0%

profile of v1, /device:TPU:0, one launch (start us, length us, event | category | flops | bytes accessed | tf_op | source)
XLA Modules:
  0.0 707.0 jit_solution(17345366208032327094)
XLA Ops:
  12.1 79.5 %all-gather.9.cloned.1.call-done = bf16[8192,512]{1,0:T(8,128)(2,1)} async-done(((bf16[256,512]{1,0:T(8,128)(2,1)}), bf16[8192,512]{1,0:T(8,128)(2,1)}) %all-gather.9.cloned.1.call-update) | async-done | bytes 8388624 | tf_op jit(solution)/shard_map/all_gather | solution.py:172
  116.3 3.2 fusion.153
  119.5 6.1 copy-done.1
  125.6 3.7 fusion.8
  130.9 8.2 %fusion.81 = bf16[8,64,512]{2,1,0:T(8,128)(2,1)S(1)} fusion(bf16[1024,8,64]{0,2,1:T(8,128)(2,1)S(1)} %bitcast.115, f32[8,512,1024]{2,1,0:T(8,128)} %copy-done.1, f32[8,512]{1,0:T(8,128)S(1)} %fusion.8, f32[8,512]{1,0:T(8,128)S(1)} %get-tuple-element.67), kind=kOutput, calls=%fused_computation.108 | convolution fusion | flops 549715968 | bytes 18382848 | tf_op jit(solution)/shard_map/hqk,khe->qhe/dot_general | solution.py:99
  144.6 4.5 fusion.155
  149.1 5.7 copy-done.2
  154.8 3.7 fusion.9
  160.1 8.0 %fusion.80 = bf16[8,64,512]{2,1,0:T(8,128)(2,1)S(1)} fusion(bf16[1024,8,64]{0,2,1:T(8,128)(2,1)S(1)} %bitcast.117, f32[8,512,1024]{2,1,0:T(8,128)} %copy-done.2, f32[8,512]{1,0:T(8,128)S(1)} %fusion.9, f32[8,512]{1,0:T(8,128)S(1)} %get-tuple-element.71), kind=kOutput, calls=%fused_computation.107 | convolution fusion | flops 549715968 | bytes 18382848 | tf_op jit(solution)/shard_map/hqk,khe->qhe/dot_general | solution.py:99
  179.5 3.8 fusion.158
  192.7 9.3 %fusion.163 = f32[8,512,1024]{2,1,0:T(8,128)} fusion(bf16[512,8,64]{0,2,1:T(8,128)(2,1)S(1)} %bitcast.119, bf16[1024,8,64]{0,2,1:T(8,128)(2,1)} %bitcast.118), kind=kOutput, calls=%fused_computation.238 | convolution fusion | flops 536870912 | bytes 18350080 | tf_op jit(solution)/shard_map/qhe,khe->hqk/dot_general | solution.py:108
  202.0 30.6 %convert_reduce_fusion.4 = (f32[8,64]{1,0:T(8,128)S(1)}, bf16[8,64,512]{2,1,0:T(8,128)(2,1)}) fusion(bf16[1024,8,64]{0,2,1:T(8,128)(2,1)} %bitcast.126, f32[8,512,1024]{2,1,0:T(8,128)} %fusion.163, f32[8,512,1024]{2,1,0:T(8,128)} %copy-done.2, f32[8,512]{1,0:T(8,128)S(1)} %log_add_fusion.1), kind=kOutput, calls=%fused_computation.127 | convolution fusion | flops 567022080 | bytes 35145728 | tf_op jit(solution)/shard_map/hqk,khe->qhe/dot_general | solution.py:113
  244.6 9.3 %fusion.164 = f32[8,512,1024]{2,1,0:T(8,128)} fusion(bf16[512,8,64]{0,2,1:T(8,128)(2,1)S(1)} %bitcast.121, bf16[1024,8,64]{0,2,1:T(8,128)(2,1)} %bitcast.116), kind=kOutput, calls=%fused_computation.239 | convolution fusion | flops 536870912 | bytes 18350080 | tf_op jit(solution)/shard_map/qhe,khe->hqk/dot_general | solution.py:108
  253.9 30.9 %fusion.19 = f32[8,64,1024]{2,1,0:T(8,128)} fusion(bf16[512,8,64]{0,2,1:T(8,128)(2,1)} %bitcast.136, f32[8,512,1024]{2,1,0:T(8,128)} %fusion.164, f32[8,512,1024]{2,1,0:T(8,128)} %copy-done.1, f32[8,512]{1,0:T(8,128)S(1)} %log_add_fusion), kind=kOutput, calls=%fused_computation.22 | convolution fusion | flops 566236160 | bytes 36192256 | tf_op jit(solution)/shard_map/hqk,qhe->khe/dot_general | solution.py:116
  284.9 10.8 %fusion.24 = f32[8,64,1024]{2,1,0:T(8,128)} fusion(bf16[512,8,64]{0,2,1:T(8,128)(2,1)} %bitcast.122, f32[8,512,1024]{2,1,0:T(8,128)} %copy-done.1, f32[8,512]{1,0:T(8,128)S(1)} %log_add_fusion), kind=kOutput, calls=%fused_computation.24 | convolution fusion | flops 545259520 | bytes 19415040 | tf_op jit(solution)/shard_map/hqk,qhe->khe/dot_general | solution.py:119
  295.7 30.9 %fusion.13 = f32[8,64,1024]{2,1,0:T(8,128)} fusion(bf16[512,8,64]{0,2,1:T(8,128)(2,1)} %bitcast.138, f32[8,512,1024]{2,1,0:T(8,128)} %fusion.163, f32[8,512,1024]{2,1,0:T(8,128)} %copy-done.2, f32[8,512]{1,0:T(8,128)S(1)} %log_add_fusion.1), kind=kOutput, calls=%fused_computation.20 | convolution fusion | flops 566236160 | bytes 36192256 | tf_op jit(solution)/shard_map/hqk,qhe->khe/dot_general | solution.py:116
  326.7 10.7 %fusion.26 = f32[8,64,1024]{2,1,0:T(8,128)} fusion(bf16[512,8,64]{0,2,1:T(8,128)(2,1)} %bitcast.120, f32[8,512,1024]{2,1,0:T(8,128)} %copy-done.2, f32[8,512]{1,0:T(8,128)S(1)} %log_add_fusion.1), kind=kOutput, calls=%fused_computation.25 | convolution fusion | flops 545259520 | bytes 19415040 | tf_op jit(solution)/shard_map/hqk,qhe->khe/dot_general | solution.py:119
  337.5 30.8 %convert_reduce_fusion.6 = (f32[8,64]{1,0:T(8,128)S(1)}, bf16[8,64,512]{2,1,0:T(8,128)(2,1)}) fusion(bf16[1024,8,64]{0,2,1:T(8,128)(2,1)} %bitcast.124, f32[8,512,1024]{2,1,0:T(8,128)} %fusion.164, f32[8,512,1024]{2,1,0:T(8,128)} %copy-done.1, f32[8,512]{1,0:T(8,128)S(1)} %log_add_fusion), kind=kOutput, calls=%fused_computation.129 | convolution fusion | flops 567022080 | bytes 35145728 | tf_op jit(solution)/shard_map/hqk,khe->qhe/dot_general | solution.py:113
  390.0 5.0 convolution_dynamic-update-slice_fusion.1
  395.1 5.5 convolution_dynamic-update-slice_fusion
  401.4 5.0 fusion.67
  415.2 166.4 %reduce-scatter.14.cloned.1.call-done = f32[256,512]{1,0:T(8,128)} async-done(((f32[8192,512]{1,0:T(8,128)}), f32[256,512]{1,0:T(8,128)}) %reduce-scatter.14.cloned.1.call-update) | async-done | bytes 524304 | tf_op jit(solution)/shard_map/reduce_scatter | solution.py:301
  595.3 59.4 %psum.7 = f32[8704]{0:T(1024)S(1)} all-reduce(f32[8704]{0:T(1024)S(1)} %constant_dynamic-update-slice_fusion.10), channel_id=1, replica_groups=mesh['dp'=16,'stream'=2] {'dp','stream'}, use_global_device_ids=true, to_apply=%region_38.39 | all-reduce | flops 8704 | bytes 69632 | tf_op jit(solution)/shard_map/psum | solution.py:302
  662.3 16.8 %collective-permute-done.2 = f32[512,512]{1,0:T(8,128)S(1)} collective-permute-done((f32[512,512]{1,0:T(8,128)S(1)}, f32[512,512]{1,0:T(8,128)S(1)}, u32[]{:S(2)}, u32[]{:S(2)}) %collective-permute-start.2) | collective-permute-done | bytes 1048608 | tf_op jit(solution)/shard_map/ppermute | solution.py:28
  (198 shorter events, 142.5 us)
Async XLA Ops:
  7.2 89.6 %copy-start = (bf16[512,512]{1,0:T(8,128)(2,1)S(1)}, bf16[512,512]{1,0:T(8,128)(2,1)}, u32[]{:S(2)}) copy-start(bf16[512,512]{1,0:T(8,128)(2,1)} %param.14) | copy-start | bytes 1572868
  7.2 84.5 %all-gather.9.cloned.1.call-start = ((), (), s32[]{:S(2)}) async-start(), calls=%async_computation.5 | async-start | bytes 8650752 | tf_op jit(solution)/shard_map/all_gather | solution.py:172
  9.1 105.5 %all-gather.13.cloned.1.call-start = ((), (), s32[]{:S(2)}) async-start(), calls=%async_computation.7 | async-start | bytes 1572864 | tf_op jit(solution)/shard_map/all_gather | solution.py:183
  94.2 35.2 %all-gather.11.cloned.1.call-start = ((), (), s32[]{:S(2)}) async-start(), calls=%async_computation.6 | async-start | bytes 1572864 | tf_op jit(solution)/shard_map/all_gather | solution.py:184
  96.7 44.3 %all-gather.17.cloned.1.call-start = ((), (), s32[]{:S(2)}) async-start(), calls=%async_computation.9 | async-start | bytes 1572864 | tf_op jit(solution)/shard_map/all_gather | solution.py:185
  99.1 59.5 %all-gather.15.cloned.1.call-start = ((), (), s32[]{:S(2)}) async-start(), calls=%async_computation.8 | async-start | bytes 1572864 | tf_op jit(solution)/shard_map/all_gather | solution.py:186
  112.9 258.0 %reduce-scatter.6.cloned.1.call-start = ((), (), s32[]{:S(2)}) async-start(), calls=%async_computation.10 | async-start | bytes 3145728 | tf_op jit(solution)/shard_map/reduce_scatter | solution.py:247
  114.6 14.7 %copy-start.22 = (bf16[512,512]{0,1:T(8,128)(2,1)}, bf16[512,512]{0,1:T(8,128)(2,1)S(1)}, u32[]{:S(2)}) copy-start(bf16[512,512]{0,1:T(8,128)(2,1)S(1)} %fusion.77) | copy-start | bytes 1572868
  142.6 15.9 %copy-start.15 = (bf16[1024,512]{0,1:T(8,128)(2,1)}, bf16[1024,512]{0,1:T(8,128)(2,1)S(1)}, u32[]{:S(2)}) copy-start(bf16[1024,512]{0,1:T(8,128)(2,1)S(1)} %copy.63) | copy-start | bytes 3145732
  144.6 13.9 %copy-start.23 = (bf16[512,512]{0,1:T(8,128)(2,1)}, bf16[512,512]{0,1:T(8,128)(2,1)S(1)}, u32[]{:S(2)}) copy-start(bf16[512,512]{0,1:T(8,128)(2,1)S(1)} %fusion.79) | copy-start | bytes 1572868
  160.1 15.1 %copy-start.17 = (bf16[512,512]{1,0:T(8,128)(2,1)S(1)}, bf16[512,512]{1,0:T(8,128)(2,1)}, u32[]{:S(2)}) copy-start(bf16[512,512]{1,0:T(8,128)(2,1)} %param.15) | copy-start | bytes 1572868
  168.1 15.2 %copy-start.20 = (bf16[8,64,512]{2,1,0:T(8,128)(2,1)}, bf16[8,64,512]{2,1,0:T(8,128)(2,1)S(1)}, u32[]{:S(2)}) copy-start(bf16[8,64,512]{2,1,0:T(8,128)(2,1)S(1)} %fusion.80) | copy-start | bytes 1572868
  284.8 88.8 %reduce-scatter.8.cloned.1.call-start = ((), (), s32[]{:S(2)}) async-start(), calls=%async_computation.11 | async-start | bytes 3145728 | tf_op jit(solution)/shard_map/reduce_scatter | solution.py:248
  295.7 86.0 %reduce-scatter.10.cloned.1.call-start = ((), (), s32[]{:S(2)}) async-start(), calls=%async_computation.12 | async-start | bytes 3145728 | tf_op jit(solution)/shard_map/reduce_scatter | solution.py:249
  326.6 57.9 %reduce-scatter.12.cloned.1.call-start = ((), (), s32[]{:S(2)}) async-start(), calls=%async_computation.13 | async-start | bytes 3145728 | tf_op jit(solution)/shard_map/reduce_scatter | solution.py:250
  337.4 244.2 %reduce-scatter.14.cloned.1.call-start = ((), (), s32[]{:S(2)}) async-start(), calls=%async_computation.14 | async-start | bytes 17301504 | tf_op jit(solution)/shard_map/reduce_scatter | solution.py:301
  400.6 185.5 %copy-start.4 = (f32[512,512]{0,1:T(8,128)S(1)}, f32[512,512]{0,1:T(8,128)}, u32[]{:S(2)}) copy-start(f32[512,512]{0,1:T(8,128)} %copy-done.3) | copy-start | bytes 3145732
  406.4 188.7 %copy-start.7 = (f32[512,512]{0,1:T(8,128)S(1)}, f32[512,512]{0,1:T(8,128)}, u32[]{:S(2)}) copy-start(f32[512,512]{0,1:T(8,128)} %reduce-scatter.12.cloned.1.call-done) | copy-start | bytes 3145732
  408.7 253.0 %copy-start.24 = (f32[8704]{0:T(1024)S(1)}, f32[8704]{0:T(1024)}, u32[]{:S(2)}) copy-start(f32[8704]{0:T(1024)} %param.22) | copy-start | bytes 104452
  408.7 253.0 %copy-start.25 = (f32[8704]{0:T(1024)S(1)}, f32[8704]{0:T(1024)}, u32[]{:S(2)}) copy-start(f32[8704]{0:T(1024)} %param.24) | copy-start | bytes 104452
  408.7 253.0 %copy-start.26 = (f32[8704]{0:T(1024)S(1)}, f32[8704]{0:T(1024)}, u32[]{:S(2)}) copy-start(f32[8704]{0:T(1024)} %param.23) | copy-start | bytes 104452
  585.7 6.9 collective-permute-start
  594.4 60.3 %collective-permute-start.1 = (f32[512,512]{1,0:T(8,128)S(1)}, f32[512,512]{1,0:T(8,128)}, u32[]{:S(2)}, u32[]{:S(2)}) collective-permute-start(f32[512,512]{1,0:T(8,128)S(1)} %select_add_fusion.7), channel_id=1, source_target_pairs={{0,2},{2,0},{1,3},{3,1},{4,6},{6,4},{5,7},{7,5},{8,10},{10,8},{9,1... | collective-permute-start | bytes 3145736 | tf_op jit(solution)/shard_map/ppermute | solution.py:28
  655.0 24.2 %collective-permute-start.2 = (f32[512,512]{1,0:T(8,128)S(1)}, f32[512,512]{1,0:T(8,128)S(1)}, u32[]{:S(2)}, u32[]{:S(2)}) collective-permute-start(f32[512,512]{1,0:T(8,128)S(1)} %select_add_fusion.6), channel_id=1, source_target_pairs={{0,4},{4,0},{1,5},{5,1},{2,6},{6,2},{3,7},{7,3},{8,12},{12,8},{9,1... | collective-permute-start | bytes 3145736 | tf_op jit(solution)/shard_map/ppermute | solution.py:28
  (17 other events, 93.6 us)
Sparse Core Ops, SparseCore 0:
  11.4 80.1 all-gather.8
  94.3 7.6 all-gather.12
  104.1 10.1 all-gather.10
  116.3 10.1 all-gather.16
  128.5 10.1 all-gather.14
  285.0 7.8 reduce-scatter.5
  295.8 10.2 reduce-scatter.7
  326.7 7.8 reduce-scatter.9
  337.5 10.1 reduce-scatter.11
  400.7 180.9 reduce-scatter.13

commit v2 on v1

v2 whole, which is shorter than its diff:
```python
import functools

import jax
import jax.numpy as jnp
from jax import lax
from jax.experimental import pallas as pl
from jax.experimental.pallas import tpu as pltpu
from jax.sharding import PartitionSpec as P

D = 512
HEADS = 8
HEAD = 64
FF = 2048
ROWS = 512
KEYS = 1024
CHUNK = 256
BF = jnp.bfloat16
F32 = jnp.float32
SCALE = HEAD ** (-0.5)
LOG2E = 1.4426950408889634
MESH = pl.DeviceIdType.MESH

NS_A = 3.4445
NS_B = -4.775
NS_C = 2.0315
MUON_RATE = 0.8
ADAM_RATE = 0.2
ADAM_DECAY = 0.01
HIGH = lax.Precision.HIGHEST


def nn(left_mat, right_mat):
    return lax.dot_general(
        left_mat, right_mat, (((1,), (0,)), ((), ())), preferred_element_type=F32
    )


def nt(left_mat, right_mat):
    return lax.dot_general(
        left_mat, right_mat, (((1,), (1,)), ((), ())), preferred_element_type=F32
    )


def tn(left_mat, right_mat):
    return lax.dot_general(
        left_mat, right_mat, (((0,), (0,)), ((), ())), preferred_element_type=F32
    )


def norm_forward(values, gain_vec, shift_vec):
    center = values - jnp.mean(values, axis=-1, keepdims=True)
    spread = lax.rsqrt(jnp.mean(center * center, axis=-1, keepdims=True) + 1e-05)
    normed = center * spread
    return normed * gain_vec + shift_vec, normed, spread


def norm_backward(normed, spread, gain_vec, grad_out):
    grad_gain = jnp.sum(grad_out * normed, axis=0, keepdims=True)
    grad_shift = jnp.sum(grad_out, axis=0, keepdims=True)
    scaled = grad_out * gain_vec
    grad_in = spread * (
        scaled
        - jnp.mean(scaled, axis=-1, keepdims=True)
        - normed * jnp.mean(scaled * normed, axis=-1, keepdims=True)
    )
    return grad_in, grad_gain, grad_shift


def column_sum(values):
    return jnp.sum(values.astype(F32), axis=0, keepdims=True)


def half_lanes(values, sub):
    lane = lax.broadcasted_iota(jnp.int32, values.shape, 1)
    keep = lane < HEAD if sub == 0 else lane >= HEAD
    return jnp.where(keep, values, jnp.zeros_like(values))


def attend_forward(q_ref, k_ref, value_t, bias, probs, mixed_t):
    def pair_body(pair, carry):
        lanes = pl.ds(pl.multiple_of(pair * 128, 128), 128)
        keys = k_ref[:, lanes]
        for sub in range(2):
            head_rows = pl.ds(pl.multiple_of(pair * 128 + sub * HEAD, HEAD), HEAD)
            for begin in range(0, ROWS, CHUNK):
                cols = slice(begin, begin + CHUNK)
                scores = nt(keys, half_lanes(q_ref[cols, lanes], sub))
                scores = scores * (SCALE * LOG2E) + bias[:, cols]
                expo = jnp.exp2(scores - jnp.max(scores, axis=0, keepdims=True))
                total = jnp.sum(expo, axis=0, keepdims=True)
                low = (expo * (1.0 / total)).astype(BF)
                probs[pair * 2 + sub, :, cols] = low
                mixed_t[head_rows, cols] = nn(value_t[head_rows, :], low).astype(BF)
        return carry

    lax.fori_loop(0, HEADS // 2, pair_body, 0)


def attend_backward(q_ref, k_t, v_ref, grad_t, mixed_t, probs, dq_t, dk_ref, dv_ref):
    def pair_body(pair, carry):
        lanes = pl.ds(pl.multiple_of(pair * 128, 128), 128)
        values = v_ref[:, lanes]
        sum_k = None
        sum_v = None
        for sub in range(2):
            head_rows = pl.ds(pl.multiple_of(pair * 128 + sub * HEAD, HEAD), HEAD)
            for begin in range(0, ROWS, CHUNK):
                cols = slice(begin, begin + CHUNK)
                grad = grad_t[head_rows, cols]
                inner = jnp.sum(
                    grad.astype(F32) * mixed_t[head_rows, cols].astype(F32), axis=0, keepdims=True
                )
                zero = jnp.zeros_like(grad)
                grad_pair = jnp.concatenate([grad, zero] if sub == 0 else [zero, grad], axis=0)
                grad_probs = nn(values, grad_pair)
                low = probs[pair * 2 + sub, :, cols]
                grad_scores = (low.astype(F32) * (grad_probs - inner)).astype(BF)
                dq_t[head_rows, cols] = (nn(k_t[head_rows, :], grad_scores) * SCALE).astype(BF)
                part_k = nn(grad_scores, half_lanes(q_ref[cols, lanes], sub))
                part_v = nn(low, grad_pair.T)
                sum_k = part_k if sum_k is None else sum_k + part_k
                sum_v = part_v if sum_v is None else sum_v + part_v
        dk_ref[:, lanes] = (sum_k * SCALE).astype(dk_ref.dtype)
        dv_ref[:, lanes] = sum_v.astype(dv_ref.dtype)
        return carry

    lax.fori_loop(0, HEADS // 2, pair_body, 0)


def layer_kernel(
    tok, mem, cot, meta, vec, w,
    out_ref, igrad_ref, mgrad_ref, g_ref, gv_ref,
    keys, metas, bias, probs_s, probs_c, flip, q_ref, cq_ref, attn_t, cross_t, grad_t, dq_t,
    parts, arrived, res_a, res_b, res_c,
    send_sem, recv_sem, meta_sem,
):
    core = lax.axis_index("stream")
    other = 1 - core
    own = pl.ds(pl.multiple_of(core * ROWS, ROWS), ROWS)
    theirs = pl.ds(pl.multiple_of(other * ROWS, ROWS), ROWS)

    def swap(src, dst, index, sems=(send_sem, recv_sem)):
        return pltpu.make_async_remote_copy(
            src_ref=src, dst_ref=dst, send_sem=sems[0].at[index], recv_sem=sems[1].at[index],
            device_id={"stream": other}, device_id_type=MESH,
        )

    barrier = pltpu.get_barrier_semaphore()
    pl.semaphore_signal(barrier, inc=1, device_id={"stream": other}, device_id_type=MESH)
    pl.semaphore_wait(barrier, 1)

    def weight(index):
        return w[index * D : (index + 1) * D, :]

    def vector(index):
        return vec[index : index + 1, :]

    def wide(index):
        return slice(index * D, (index + 1) * D)

    meta_copy = pltpu.make_async_remote_copy(
        src_ref=meta, dst_ref=metas, send_sem=meta_sem.at[0], recv_sem=meta_sem.at[1],
        device_id={"stream": other}, device_id_type=MESH,
    )
    meta_copy.start()
    hid, _, _ = norm_forward(tok[...].astype(F32), vector(0), vector(1))
    hid = hid.astype(BF)
    keys[0, own, :] = nn(hid, weight(1)).astype(BF)
    copies = []
    for index in range(4):
        copies.append(swap(keys.at[index, own, :], keys.at[index, own, :], index))
    copies[0].start()
    keys[1, own, :] = (nn(hid, weight(2)) + vector(7)).astype(BF)
    copies[1].start()
    q_ref[...] = (nn(hid, weight(0)) + vector(6)).astype(BF)
    keys[2, own, :] = nn(mem[...], weight(5)).astype(BF)
    copies[2].start()
    keys[3, own, :] = (nn(mem[...], weight(6)) + vector(10)).astype(BF)
    copies[3].start()

    meta_copy.wait()
    row = lax.broadcasted_iota(jnp.int32, (ROWS, ROWS), 0)
    col = lax.broadcasted_iota(jnp.int32, (ROWS, ROWS), 1)

    def fill_bias(with_priority):
        for rows, source, own_half in ((own, meta, True), (theirs, metas, False)):
            turned = source[...].T
            visible = turned[:, 0:1] == meta[2:3, :]
            if with_priority:
                visible = visible & (turned[:, 1:2] < meta[3:4, :])
            if own_half:
                visible = visible | (row == col)
            bias[rows, :] = jnp.where(visible, 0.0, -1e30)

    fill_bias(True)
    copies[0].wait()
    copies[1].wait()
    flip[...] = keys[1].T
    attend_forward(q_ref, keys.at[0], flip, bias, probs_s, attn_t)
    res_one = tok[...].astype(F32) + nn(attn_t[...].T, weight(3)) + vector(8)
    res_a[...] = res_one
    hid, _, _ = norm_forward(res_one, vector(2), vector(3))
    cq_ref[...] = (nn(hid.astype(BF), weight(4)) + vector(9)).astype(BF)
    fill_bias(False)
    copies[2].wait()
    copies[3].wait()
    flip[...] = keys[3].T
    attend_forward(cq_ref, keys.at[2], flip, bias, probs_c, cross_t)
    res_two = res_a[...] + nn(cross_t[...].T, weight(7)) + vector(11)
    res_b[...] = res_two
    hid, _, _ = norm_forward(res_two, vector(4), vector(5))
    grad_t[...] = hid.astype(BF)
    res_c[...] = jnp.zeros((ROWS, D), F32)
    out_sum = res_two + vector(12)
    igrad_ref[...] = out_sum
    gv_ref[12:13, :] = column_sum(cot[...])

    def ffn_body(part, carry):
        rows_in = pl.ds(pl.multiple_of(8 * D + part * D, D), D)
        rows_out = pl.ds(pl.multiple_of(8 * D + FF + part * D, D), D)
        w_in = w[rows_in, :]
        w_out = w[rows_out, :]
        h_three = grad_t[...]
        pre = nt(h_three, w_in) + vec[pl.ds(13 + part, 1), :]
        hidden = jnp.maximum(pre, 0.0).astype(BF)
        igrad_ref[...] += nn(hidden, w_out)
        grad_pre = jnp.where(pre > 0, nt(cot[...], w_out), 0.0).astype(BF)
        res_c[...] += nn(grad_pre, w_in)
        gv_ref[pl.ds(13 + part, 1), :] = column_sum(grad_pre)
        g_ref[rows_in, :] = tn(grad_pre, h_three).astype(BF)
        g_ref[rows_out, :] = tn(hidden, cot[...]).astype(BF)
        return carry

    lax.fori_loop(0, FF // D, ffn_body, 0)
    out_ref[...] = igrad_ref[...].astype(BF)

    _, normed, spread = norm_forward(res_b[...], vector(4), vector(5))
    grad_in, gv_ref[4:5, :], gv_ref[5:6, :] = norm_backward(normed, spread, vector(4), res_c[...])
    grad_res = cot[...].astype(F32) + grad_in
    res_b[...] = grad_res
    gv_ref[11:12, :] = column_sum(grad_res)
    grad_low = grad_res.astype(BF)
    g_ref[wide(7), :] = nn(cross_t[...], grad_low).astype(BF)
    grad_t[...] = nt(weight(7), grad_low).astype(BF)
    flip[...] = keys[2].T
    attend_backward(
        cq_ref, flip, keys.at[3], grad_t, cross_t, probs_c, dq_t, parts.at[2], parts.at[3]
    )
    back = [swap(parts.at[index, theirs, :], arrived.at[index], 4 + index) for index in range(4)]
    back[2].start()
    back[3].start()
    grad_cq = dq_t[...].T
    gv_ref[9:10, :] = column_sum(grad_cq)
    hid, normed, spread = norm_forward(res_a[...], vector(2), vector(3))
    g_ref[wide(4), :] = tn(hid.astype(BF), grad_cq).astype(BF)
    grad_in, gv_ref[2:3, :], gv_ref[3:4, :] = norm_backward(
        normed, spread, vector(2), nt(grad_cq, weight(4))
    )
    grad_res = res_b[...] + grad_in
    res_b[...] = grad_res
    gv_ref[8:9, :] = column_sum(grad_res)
    grad_low = grad_res.astype(BF)
    g_ref[wide(3), :] = nn(attn_t[...], grad_low).astype(BF)
    grad_t[...] = nt(weight(3), grad_low).astype(BF)
    flip[...] = keys[0].T
    attend_backward(
        q_ref, flip, keys.at[1], grad_t, attn_t, probs_s, dq_t, parts.at[0], parts.at[1]
    )
    back[0].start()
    back[1].start()

    def summed(index):
        back[index].wait()
        return (parts[index, own, :].astype(F32) + arrived[index].astype(F32)).astype(BF)

    grad_mk = summed(2)
    grad_mv = summed(3)
    gv_ref[10:11, :] = column_sum(grad_mv)
    mgrad_ref[...] = nt(grad_mk, weight(5)) + nt(grad_mv, weight(6))
    g_ref[wide(5), :] = tn(mem[...], grad_mk).astype(BF)
    g_ref[wide(6), :] = tn(mem[...], grad_mv).astype(BF)
    hid, normed, spread = norm_forward(tok[...].astype(F32), vector(0), vector(1))
    hid = hid.astype(BF)
    grad_q = dq_t[...].T
    gv_ref[6:7, :] = column_sum(grad_q)
    g_ref[wide(0), :] = tn(hid, grad_q).astype(BF)
    grad_h = nt(grad_q, weight(0))
    grad_k = summed(0)
    g_ref[wide(1), :] = tn(hid, grad_k).astype(BF)
    grad_h = grad_h + nt(grad_k, weight(1))
    grad_v = summed(1)
    gv_ref[7:8, :] = column_sum(grad_v)
    g_ref[wide(2), :] = tn(hid, grad_v).astype(BF)
    grad_h = grad_h + nt(grad_v, weight(2))
    grad_in, gv_ref[0:1, :], gv_ref[1:2, :] = norm_backward(normed, spread, vector(0), grad_h)
    igrad_ref[...] = res_b[...] + grad_in


def layer_call(tok, mem, cot, meta, vec, w):
    shape = jax.ShapeDtypeStruct
    vmem = pl.BlockSpec(memory_space=pltpu.VMEM)
    return pl.pallas_call(
        layer_kernel,
        out_shape=[
            shape((ROWS, D), BF), shape((ROWS, D), F32), shape((ROWS, D), F32),
            shape(w.shape, BF), shape(vec.shape, F32),
        ],
        in_specs=[vmem] * 6,
        out_specs=[vmem] * 5,
        scratch_shapes=[
            pltpu.VMEM((4, KEYS, D), BF),
            pltpu.VMEM((8, ROWS), jnp.int32),
            pltpu.VMEM((KEYS, ROWS), F32),
            pltpu.VMEM((HEADS, KEYS, ROWS), BF),
            pltpu.VMEM((HEADS, KEYS, ROWS), BF),
            pltpu.VMEM((D, KEYS), BF),
            pltpu.VMEM((ROWS, D), BF),
            pltpu.VMEM((ROWS, D), BF),
            pltpu.VMEM((D, ROWS), BF),
            pltpu.VMEM((D, ROWS), BF),
            pltpu.VMEM((D, ROWS), BF),
            pltpu.VMEM((D, ROWS), BF),
            pltpu.VMEM((4, KEYS, D), BF),
            pltpu.VMEM((4, ROWS, D), BF),
            pltpu.VMEM((ROWS, D), F32),
            pltpu.VMEM((ROWS, D), F32),
            pltpu.VMEM((ROWS, D), F32),
            pltpu.SemaphoreType.DMA((8,)),
            pltpu.SemaphoreType.DMA((8,)),
            pltpu.SemaphoreType.DMA((2,)),
        ],
        compiler_params=pltpu.CompilerParams(
            collective_id=0, has_side_effects=True, vmem_limit_bytes=63 * 1024 * 1024
        ),
        cost_estimate=pl.CostEstimate(
            flops=22_000_000_000, bytes_accessed=24_000_000, transcendentals=8_000_000
        ),
    )(tok, mem, cot, meta, vec, w)


def partner(block, axis, stride):
    count = lax.axis_size(axis)
    route = []
    for low in range(count):
        high = low | 1 << stride
        if high != low and high < count:
            route += [(low, high), (high, low)]
    return lax.ppermute(block, axis, route)


def high_dot(left_mat, right_mat):
    return jnp.dot(left_mat, right_mat, precision=lax.Precision.HIGH)


def exact_lead(left_mat, right_mat):
    return lax.dot_general(left_mat, right_mat, (((0,), (0,)), ((), ())), precision=HIGH)


def per_device(
    tokens,
    memory,
    cotangent,
    segments,
    padding,
    priority,
    threshold,
    master,
    momentum,
    vectors,
    vec_first,
    vec_second,
    step_count,
):
    low_all = lax.all_gather(master.astype(BF), ("dp", "stream"), axis=0, tiled=True)
    meta = jnp.stack([jnp.where(padding == 0, segments, -1), priority, segments, threshold] * 2)
    layer_out, input_grad, memory_grad, grad_all, vec_local = layer_call(
        tokens, memory, cotangent, meta, vectors.reshape(-1, D), low_all
    )
    grad_rows = lax.psum_scatter(
        grad_all, ("dp", "stream"), scatter_dimension=0, tiled=True
    ).astype(F32)
    grad_vec = lax.psum(vec_local.reshape(-1), ("dp", "stream"))
    opt_rows = master.shape[0]
    device_index = lax.axis_index(("dp", "stream"))
    start_row = device_index * opt_rows
    in_ffn = start_row >= 8 * D
    att_bits = (D // opt_rows).bit_length() - 1
    ffn_bits = (FF // opt_rows).bit_length() - 1
    own_bits = jnp.where(in_ffn, ffn_bits, att_bits)
    new_momentum = 0.5 * momentum + grad_rows

    def gram_total(partial_value):
        for bit_pos in range(ffn_bits):
            other = partner(partial_value, ("dp", "stream"), bit_pos)
            partial_value = partial_value + jnp.where(bit_pos < own_bits, other, 0.0)
        return partial_value

    gram_first = gram_total(exact_lead(new_momentum, new_momentum))
    divisor = jnp.sqrt(jnp.trace(gram_first)) + 1e-07
    gram = gram_first / (divisor * divisor)
    unit = jnp.eye(D, dtype=jnp.float32)
    chain = None
    for turn in range(5):
        poly = NS_A * unit + NS_B * gram + NS_C * high_dot(gram, gram)
        chain = poly if chain is None else high_dot(chain, poly)
        if turn < 4:
            gram = high_dot(high_dot(gram, poly), poly)
    current = high_dot(new_momentum / divisor, chain)
    rate = MUON_RATE * jnp.where(in_ffn, (FF / D) ** 0.5, 1.0)
    new_master = master - rate * current
    count = step_count[0].astype(jnp.float32)
    new_first = 0.5 * vec_first + 0.5 * grad_vec
    new_second = 0.999 * vec_second + 0.001 * grad_vec * grad_vec
    first_fix = new_first / (1.0 - jnp.power(0.5, count))
    second_fix = new_second / (1.0 - jnp.power(0.999, count))
    new_vectors = vectors - ADAM_RATE * (
        first_fix / (jnp.sqrt(second_fix) + 1e-08) + ADAM_DECAY * vectors
    )
    return (
        layer_out,
        input_grad,
        memory_grad,
        new_momentum,
        new_master,
        new_vectors,
        new_first,
        new_second,
    )


def solution(mesh):
    return jax.shard_map(
        per_device,
        mesh=mesh,
        in_specs=(
            P(("dp", "stream"), None),
            P(("dp", "stream"), None),
            P(("dp", "stream"), None),
            P(("dp", "stream")),
            P(("dp", "stream")),
            P(("dp", "stream")),
            P(("dp", "stream")),
            P(("dp", "stream"), None),
            P(("dp", "stream"), None),
            P(),
            P(),
            P(),
            P(),
        ),
        out_specs=(
            P(("dp", "stream"), None),
            P(("dp", "stream"), None),
            P(("dp", "stream"), None),
            P(("dp", "stream"), None),
            P(("dp", "stream"), None),
            P(),
            P(),
            P(),
        ),
        check_vma=False,
    )
```

time: 713 us -> 446 us (0.63)
  matrix products: 288 us -> 22.1 us
  Pallas kernels: 0 us -> 81.3 us
  local copies, waits for them, and re-layouts: 39.6 us -> 5.59 us
  other arithmetic: 30.2 us -> 7.62 us
  blocking collectives: 65.1 us -> 55.6 us
  waiting for transfers between devices: 263 us -> 255 us
    dot_general x42 -> x0, matrix products: 267 us -> none  [the longest x2 61.7 us: attend_backward(): jnp.einsum('hqk,qhe->khe', grad_scores, split_heads(queries), preferred_e...]
    pallas_call x0 -> x1, Pallas kernels: none -> 81.3 us  [layer_call(): pl.pallas_call(layer_kernel, out_shape=[shape((ROWS, D), BF), shape((ROWS...]
    unnamed x73 -> x25, local copies, waits for them, and re-layouts: 27.6 us -> 2.79 us
    reduce_scatter x5 -> x1, waiting for transfers between devices: 166 us -> 147 us  [per_device(): lax.psum_scatter(grad_all, ('dp', 'stream'), scatter_dimension=0, tiled=T...]
    reduce_sum x12 -> x0, other arithmetic: 16.7 us -> none  [the longest x2 7.39 us: attend_forward(): row_total = jnp.sum(expo, axis=-1, keepdims=True)]
    ppermute x3, waiting for transfers between devices: 16.8 us -> 28.1 us  [partner(): return lax.ppermute(block, axis, route)]
    all_gather x5 -> x1, waiting for transfers between devices: 79.6 us -> 79.1 us  [per_device(): lax.all_gather(master.astype(BF), ('dp', 'stream'), axis=0, tiled=True)]
  transfers between devices with their start and end apart: 13 -> 5, of which waited for: 3 -> 4; matrix products, arithmetic and copies ran while one was open for 25% -> 1% of each run, Pallas kernels for 0% -> 0%
where the time goes in v2:
time: 446 us; the launch traced here: 443 us
  waiting for transfers between devices  255 us (57%)
  Pallas kernels  81.3 us (18%)
  blocking collectives  55.6 us (12%)
  matrix products  22.1 us (5%)
  between operations  16.1 us (4%)
  other arithmetic  7.62 us (2%)
  local copies, waits for them, and re-layouts  5.59 us (1%)
    reduce_scatter x1, waiting for transfers between devices, per_device(): lax.psum_scatter(grad_all, ('dp', 'stream'), scatter_dimension=0, tiled=T...  147 us
    pallas_call x1, Pallas kernels, layer_call(): pl.pallas_call(layer_kernel, out_shape=[shape((ROWS, D), BF), shape((ROWS...  81.3 us
    all_gather x1, waiting for transfers between devices, per_device(): lax.all_gather(master.astype(BF), ('dp', 'stream'), axis=0, tiled=True)  79.1 us
    psum x1, blocking collectives, per_device(): grad_vec = lax.psum(vec_local.reshape(-1), ('dp', 'stream'))  55.6 us
    ppermute x3, waiting for transfers between devices, partner(): return lax.ppermute(block, axis, route)  28.1 us
    dot_general x18, matrix products, high_dot(): return jnp.dot(left_mat, right_mat, precision=lax.Precision.HIGH)  21.1 us
  transfers between devices with their start and end apart: 5, of which 4 were waited for; matrix products, arithmetic and copies ran while one was open for 1% of the time, Pallas kernels for 0%

profile of v2, /device:TPU:0, one launch (start us, length us, event | category | flops | bytes accessed | tf_op | source)
XLA Modules:
  0.0 443.3 jit_solution(4875238625154644457)
XLA Ops:
  7.2 1.8 convert_element_type.11
  9.1 1.4 reshape.31.vec
  11.2 1.4 stack.23.meta
  12.6 79.1 %all-gather.2.cloned.1.call-done.w = bf16[8192,512]{1,0:T(8,128)(2,1)} async-done(((bf16[256,512]{1,0:T(8,128)(2,1)}), bf16[8192,512]{1,0:T(8,128)(2,1)}) %all-gather.2.cloned.1.call-update) | async-done | bytes 8388624 | tf_op jit(solution)/shard_map/all_gather | solution.py:374
  91.6 81.3 %shard_map.188 = (bf16[512,512]{1,0:T(8,128)(2,1)}, f32[512,512]{1,0:T(8,128)}, f32[512,512]{1,0:T(8,128)}, bf16[8192,512]{1,0:T(8,128)(2,1)}, f32[17,512]{1,0:T(8,128)}) custom-call(bf16[512,512]{1,0:T(8,128)(2,1)} %tok.1, bf16[512,512]{1,0:T(8,128)(2,1)} %mem.1, bf16[512,512]{1,0:T(8,128)(2,1)} %cot.1, s32[8,512]{1,0:T(8,128)} %stack.23.meta, ...), custom_call_target="tpu_custom_call" | custom-call | flops 22000001024 | bytes 24000000 | tf_op jit(solution)/shard_map/pallas_call | solution.py:302
  173.0 147.5 %reduce-scatter.2.cloned.1.call-done = bf16[256,512]{1,0:T(8,128)(2,1)} async-done(((bf16[8192,512]{1,0:T(8,128)(2,1)}), bf16[256,512]{1,0:T(8,128)(2,1)}) %reduce-scatter.2.cloned.1.call-update) | async-done | bytes 262160 | tf_op jit(solution)/shard_map/reduce_scatter | solution.py:379
  320.5 1.0 convert_add_fusion
  321.5 1.0 fusion.11
  322.6 2.8 collective-permute-done
  325.4 1.4 select_add_fusion.7
  326.9 25.3 %collective-permute-done.1 = f32[512,512]{1,0:T(8,128)} collective-permute-done((f32[512,512]{1,0:T(8,128)S(1)}, f32[512,512]{1,0:T(8,128)}, u32[]{:S(2)}, u32[]{:S(2)}) %collective-permute-start.1) | collective-permute-done | bytes 1048608 | tf_op jit(solution)/shard_map/ppermute | solution.py:348
  353.3 55.6 %psum.7 = f32[8704]{0:T(1024)S(1)} all-reduce(f32[8704]{0:T(1024)S(1)} %reshape.32), channel_id=1, replica_groups=mesh['dp'=16,'stream'=2] {'dp','stream'}, use_global_device_ids=true, to_apply=%region_2.3 | all-reduce | flops 8704 | bytes 69632 | tf_op jit(solution)/shard_map/psum | solution.py:382
  409.6 1.8 select_reduce_fusion
  412.2 3.2 fusion.5
  415.4 1.0 fusion.7
  416.4 1.0 fusion.12
  417.4 1.1 fusion.3
  419.5 1.0 fusion.13
  421.5 1.1 fusion.2
  423.6 1.0 fusion.18
  424.6 1.1 fusion.1
  426.7 1.2 fusion.21
  427.9 1.1 fusion
  432.1 1.4 fusion.4
  (44 shorter events, 11.8 us)
Async XLA Ops:
  7.2 84.5 %all-gather.2.cloned.1.call-start = ((), (), s32[]{:S(2)}) async-start(), calls=%async_computation.1 | async-start | bytes 8650752 | tf_op jit(solution)/shard_map/all_gather | solution.py:374
  9.0 311.4 %reduce-scatter.2.cloned.1.call-start = ((), (), s32[]{:S(2)}) async-start(), calls=%async_computation.2 | async-start | bytes 8650752 | tf_op jit(solution)/shard_map/reduce_scatter | solution.py:379
  172.9 147.6 %copy-start.5 = (f32[256,512]{1,0:T(8,128)S(1)}, f32[256,512]{1,0:T(8,128)}, u32[]{:S(2)}) copy-start(f32[256,512]{1,0:T(8,128)} %param.21) | copy-start | bytes 1572868
  172.9 180.4 %copy-start.8 = (f32[17,512]{1,0:T(8,128)S(1)}, f32[17,512]{1,0:T(8,128)}, u32[]{:S(2)}) copy-start(f32[17,512]{1,0:T(8,128)} %get-tuple-element.17) | copy-start | bytes 104452
  172.9 236.0 %copy-start.7 = (f32[8704]{0:T(1024)S(1)}, f32[8704]{0:T(1024)}, u32[]{:S(2)}) copy-start(f32[8704]{0:T(1024)} %param.22) | copy-start | bytes 104452
  172.9 236.0 %copy-start.9 = (f32[8704]{0:T(1024)S(1)}, f32[8704]{0:T(1024)}, u32[]{:S(2)}) copy-start(f32[8704]{0:T(1024)} %param.24) | copy-start | bytes 104452
  172.9 236.0 %copy-start.10 = (f32[8704]{0:T(1024)S(1)}, f32[8704]{0:T(1024)}, u32[]{:S(2)}) copy-start(f32[8704]{0:T(1024)} %param.23) | copy-start | bytes 104452
  321.5 110.6 %copy-start = (f32[256,512]{1,0:T(8,128)}, f32[256,512]{1,0:T(8,128)S(1)}, u32[]{:S(2)}) copy-start(f32[256,512]{1,0:T(8,128)S(1)} %convert_add_fusion) | copy-start | bytes 1572868
  322.5 2.9 collective-permute-start
  326.8 25.4 %collective-permute-start.1 = (f32[512,512]{1,0:T(8,128)S(1)}, f32[512,512]{1,0:T(8,128)}, u32[]{:S(2)}, u32[]{:S(2)}) collective-permute-start(f32[512,512]{1,0:T(8,128)S(1)} %select_add_fusion.7), channel_id=1, source_target_pairs={{0,2},{2,0},{1,3},{3,1},{4,6},{6,4},{5,7},{7,5},{8,10},{10,8},{9,1... | collective-permute-start | bytes 3145736 | tf_op jit(solution)/shard_map/ppermute | solution.py:348
  352.4 57.2 %collective-permute-start.2 = (f32[512,512]{1,0:T(8,128)S(1)}, f32[512,512]{1,0:T(8,128)S(1)}, u32[]{:S(2)}, u32[]{:S(2)}) collective-permute-start(f32[512,512]{1,0:T(8,128)S(1)} %select_add_fusion.6), channel_id=1, source_target_pairs={{0,4},{4,0},{1,5},{5,1},{2,6},{6,2},{3,7},{7,3},{8,12},{12,8},{9,1... | collective-permute-start | bytes 3145736 | tf_op jit(solution)/shard_map/ppermute | solution.py:348
  411.4 3.9 copy-start.4
  426.7 5.4 %copy-start.1 = (f32[256,512]{1,0:T(8,128)S(1)}, f32[256,512]{1,0:T(8,128)}, u32[]{:S(2)}) copy-start(f32[256,512]{1,0:T(8,128)} %param.20) | copy-start | bytes 1572868
  427.9 5.6 %copy-start.6 = (bf16[512,512]{1,0:T(8,128)(2,1)S(1)}, bf16[512,512]{1,0:T(8,128)(2,1)}, u32[]{:S(2)}) copy-start(bf16[512,512]{1,0:T(8,128)(2,1)} %get-tuple-element.31) | copy-start | bytes 1572868
  427.9 6.4 %copy-start.3 = (f32[512,512]{1,0:T(8,128)S(1)}, f32[512,512]{1,0:T(8,128)}, u32[]{:S(2)}) copy-start(f32[512,512]{1,0:T(8,128)} %get-tuple-element.32) | copy-start | bytes 3145732
  429.0 6.3 %copy-start.2 = (f32[512,512]{1,0:T(8,128)S(1)}, f32[512,512]{1,0:T(8,128)}, u32[]{:S(2)}) copy-start(f32[512,512]{1,0:T(8,128)} %get-tuple-element.33) | copy-start | bytes 3145732
Sparse Core Ops, SparseCore 0:
  11.4 80.1 all-gather.1
  173.1 147.3 reduce-scatter.1
